TPU v7x, 512 devices: a whole 4x4x16 slice. The times are simulated.
512 devices in a mesh: row: 8 (over x, core), col: 16 (over z), depth: 4 (over y).
Axes of the slice: x: 4, y: 4, z: 16, core: 2. Of those that a mesh axis runs over, the one named last changes fastest.
Arguments:
- density: float32 [4096, 4096], P('row', 'col'), as said below
- pattern: int32 [32, 32], P('row', 'col'), may hold values from 0 to 1, as said below
- branch: int32 [4], replicated, may hold values from 0 to 1, as said below
Outputs:
- purified: float32 [4096, 4096], P('row', 'col')
Inputs may be any that keep to these rules, and one draw needn't show every extreme that they name: `branch`: each entry is 0 or 1; both values occur. Each entry is 0 or 1, and pattern[i, j] = pattern[j, i]. density is symmetric: density[i, j] = density[j, i].
All inputs are finite; a program needn't handle non-finite values.
Results may differ from a plain program's by a relative error of at most 0.00026.
Values sent between devices are 32-bit elements; how exact they have to be, the bound alone decides.
No kernel may reach another device: no remote copies, remote signals or barrier semaphores. Data moves between devices by JAX's collectives and lax.ppermute only.
A program may use at most 64 MiB of HBM per device.

v0:
```python
import jax
import jax.numpy as jnp
from jax import lax
from jax.sharding import PartitionSpec as P

TILE = 128
STEPS = 4


def keep_cells(pattern):
    row_start = lax.axis_index("row") * pattern.shape[0]
    col_start = lax.axis_index("col") * pattern.shape[1]
    row_ids = lax.broadcasted_iota(jnp.int32, pattern.shape, 0) + row_start
    col_ids = lax.broadcasted_iota(jnp.int32, pattern.shape, 1) + col_start
    tile_mask = jnp.where(row_ids == col_ids, 1, pattern)
    return jnp.repeat(jnp.repeat(tile_mask, TILE, axis=0), TILE, axis=1).astype(jnp.float32)


def layer_product(current, layer):
    rows_local, cols_local = current.shape
    layers = lax.axis_size("depth")
    sub_width = cols_local // layers
    column_part = lax.dynamic_slice_in_dim(current, layer * sub_width, sub_width, 1)
    grouped = current.reshape(rows_local // cols_local, layers, sub_width, cols_local)
    row_part = lax.dynamic_index_in_dim(grouped, layer, 1, keepdims=False).reshape(-1, cols_local)
    inner_rows = lax.all_gather(row_part, "row", axis=0, tiled=True)
    return jnp.dot(
        lax.all_gather(column_part, "col", axis=1, tiled=True),
        inner_rows,
        precision=lax.Precision.HIGHEST,
        preferred_element_type=jnp.float32,
    )


def local(density, pattern, branch):
    layer = lax.axis_index("depth")
    on_pattern = keep_cells(pattern)
    current = density * on_pattern
    for step in range(STEPS):
        partial_sum = layer_product(current, layer)
        square_branch = branch[step] == 1
        squared = lax.psum(partial_sum, "depth")
        current = on_pattern * jnp.where(square_branch, squared, 2.0 * current - squared)
    return current


def solution(mesh):
    in_specs = (P("row", "col"), P("row", "col"), P())
    out_specs = P("row", "col")
    return jax.shard_map(local, mesh=mesh, in_specs=in_specs, out_specs=out_specs, check_vma=False)
```

profile of v0, /device:TPU:1, one launch (start us, length us, event | category | flops | bytes accessed | tf_op | source)
XLA Modules:
  0.0 701.4 jit_solution(16342361267251926590)
XLA Ops:
  8.0 1.1 bitcast_multiply_fusion
  10.0 0.8 copy.6
  10.9 36.0 %all-gather.11.cloned.1.call-done = f32[1024,256]{1,0:T(8,128)} async-done(((f32[128,256]{1,0:T(8,128)}), f32[1024,256]{1,0:T(8,128)}) %all-gather.11.cloned.1.call-update) | async-done | bytes 1048592 | tf_op jit(solution)/shard_map/all_gather | solution.py:26
  46.9 65.5 %all-gather.9.cloned.1.call-done = f32[512,1024]{0,1:T(8,128)} async-done(((f32[512,64]{0,1:T(8,128)}), f32[512,1024]{0,1:T(8,128)}) %all-gather.9.cloned.1.call-update) | async-done | bytes 2097168 | tf_op jit(solution)/shard_map/all_gather | solution.py:28
  112.4 6.1 fusion.6
  119.9 61.1 %all-reduce.5.cloned.1.call-done = f32[512,256]{1,0:T(8,128)} async-done(((f32[512,256]{1,0:T(8,128)}), f32[512,256]{1,0:T(8,128)}) %all-reduce.5.cloned.1.call-update) | async-done | bytes 524304 | tf_op jit(solution)/shard_map/psum | solution.py:42
  181.0 1.1 fusion
  183.0 0.8 copy.7
  183.9 33.6 %all-gather.15.cloned.1.call-done = f32[1024,256]{1,0:T(8,128)} async-done(((f32[128,256]{1,0:T(8,128)}), f32[1024,256]{1,0:T(8,128)}) %all-gather.15.cloned.1.call-update) | async-done | bytes 1048592 | tf_op jit(solution)/shard_map/all_gather | solution.py:26
  217.4 65.4 %all-gather.13.cloned.1.call-done = f32[512,1024]{0,1:T(8,128)} async-done(((f32[512,64]{0,1:T(8,128)}), f32[512,1024]{0,1:T(8,128)}) %all-gather.13.cloned.1.call-update) | async-done | bytes 2097168 | tf_op jit(solution)/shard_map/all_gather | solution.py:28
  282.8 6.1 fusion.7
  289.5 61.9 %all-reduce.7.cloned.1.call-done = f32[512,256]{1,0:T(8,128)} async-done(((f32[512,256]{1,0:T(8,128)}), f32[512,256]{1,0:T(8,128)}) %all-reduce.7.cloned.1.call-update) | async-done | bytes 524304 | tf_op jit(solution)/shard_map/psum | solution.py:42
  351.4 1.1 fusion.1
  353.4 0.8 copy.8
  354.4 33.6 %all-gather.19.cloned.1.call-done = f32[1024,256]{1,0:T(8,128)} async-done(((f32[128,256]{1,0:T(8,128)}), f32[1024,256]{1,0:T(8,128)}) %all-gather.19.cloned.1.call-update) | async-done | bytes 1048592 | tf_op jit(solution)/shard_map/all_gather | solution.py:26
  388.0 65.5 %all-gather.17.cloned.1.call-done = f32[512,1024]{0,1:T(8,128)} async-done(((f32[512,64]{0,1:T(8,128)}), f32[512,1024]{0,1:T(8,128)}) %all-gather.17.cloned.1.call-update) | async-done | bytes 2097168 | tf_op jit(solution)/shard_map/all_gather | solution.py:28
  453.5 6.1 fusion.8
  460.4 61.7 %all-reduce.9.cloned.1.call-done = f32[512,256]{1,0:T(8,128)} async-done(((f32[512,256]{1,0:T(8,128)}), f32[512,256]{1,0:T(8,128)}) %all-reduce.9.cloned.1.call-update) | async-done | bytes 524304 | tf_op jit(solution)/shard_map/psum | solution.py:42
  522.1 1.1 fusion.2
  525.0 33.6 %all-gather.23.cloned.1.call-done = f32[1024,256]{1,0:T(8,128)} async-done(((f32[128,256]{1,0:T(8,128)}), f32[1024,256]{1,0:T(8,128)}) %all-gather.23.cloned.1.call-update) | async-done | bytes 1048592 | tf_op jit(solution)/shard_map/all_gather | solution.py:26
  558.5 65.5 %all-gather.21.cloned.1.call-done = f32[512,1024]{0,1:T(8,128)} async-done(((f32[512,64]{0,1:T(8,128)}), f32[512,1024]{0,1:T(8,128)}) %all-gather.21.cloned.1.call-update) | async-done | bytes 2097168 | tf_op jit(solution)/shard_map/all_gather | solution.py:28
  624.1 6.1 fusion.9
  630.8 61.9 %all-reduce.11.cloned.1.call-done = f32[512,256]{1,0:T(8,128)} async-done(((f32[512,256]{1,0:T(8,128)}), f32[512,256]{1,0:T(8,128)}) %all-reduce.11.cloned.1.call-update) | async-done | bytes 524304 | tf_op jit(solution)/shard_map/psum | solution.py:42
  692.7 1.9 fusion.3
  (44 shorter events, 7.0 us)
Async XLA Ops:
  6.5 40.3 %all-gather.11.cloned.1.call-start = ((), (), s32[]{:S(2)}) async-start(), calls=%async_computation.1 | async-start | bytes 1179648 | tf_op jit(solution)/shard_map/all_gather | solution.py:26
  9.8 102.6 %all-gather.9.cloned.1.call-start = ((), (), s32[]{:S(2)}) async-start(), calls=%async_computation | async-start | bytes 2228224 | tf_op jit(solution)/shard_map/all_gather | solution.py:28
  10.8 107.7 %copy-start.1 = (s32[4]{0:T(128)S(1)}, s32[4]{0:T(128)}, u32[]{:S(2)}) copy-start(s32[4]{0:T(128)} %param.5) | copy-start | bytes 52
  10.8 170.2 %copy-start = (f32[512,256]{1,0:T(8,128)S(1)}, f32[512,256]{1,0:T(8,128)}, u32[]{:S(2)}) copy-start(f32[512,256]{1,0:T(8,128)} %param.3) | copy-start | bytes 1572868
  10.8 170.1 %all-reduce.5.cloned.1.call-start = ((), (), s32[]{:S(2)}) async-start(), calls=%async_computation.2 | async-start | bytes 1048576 | tf_op jit(solution)/shard_map/psum | solution.py:42
  118.5 98.9 %all-gather.15.cloned.1.call-start = ((), (), s32[]{:S(2)}) async-start(), calls=%async_computation.4 | async-start | bytes 1179648 | tf_op jit(solution)/shard_map/all_gather | solution.py:26
  182.8 100.0 %all-gather.13.cloned.1.call-start = ((), (), s32[]{:S(2)}) async-start(), calls=%async_computation.3 | async-start | bytes 2228224 | tf_op jit(solution)/shard_map/all_gather | solution.py:28
  183.8 167.6 %all-reduce.7.cloned.1.call-start = ((), (), s32[]{:S(2)}) async-start(), calls=%async_computation.5 | async-start | bytes 1048576 | tf_op jit(solution)/shard_map/psum | solution.py:42
  288.9 99.1 %all-gather.19.cloned.1.call-start = ((), (), s32[]{:S(2)}) async-start(), calls=%async_computation.7 | async-start | bytes 1179648 | tf_op jit(solution)/shard_map/all_gather | solution.py:26
  353.2 100.3 %all-gather.17.cloned.1.call-start = ((), (), s32[]{:S(2)}) async-start(), calls=%async_computation.6 | async-start | bytes 2228224 | tf_op jit(solution)/shard_map/all_gather | solution.py:28
  354.2 167.9 %all-reduce.9.cloned.1.call-start = ((), (), s32[]{:S(2)}) async-start(), calls=%async_computation.8 | async-start | bytes 1048576 | tf_op jit(solution)/shard_map/psum | solution.py:42
  459.6 98.9 %all-gather.23.cloned.1.call-start = ((), (), s32[]{:S(2)}) async-start(), calls=%async_computation.10 | async-start | bytes 1179648 | tf_op jit(solution)/shard_map/all_gather | solution.py:26
  523.9 100.1 %all-gather.21.cloned.1.call-start = ((), (), s32[]{:S(2)}) async-start(), calls=%async_computation.9 | async-start | bytes 2228224 | tf_op jit(solution)/shard_map/all_gather | solution.py:28
  524.9 167.7 %all-reduce.11.cloned.1.call-start = ((), (), s32[]{:S(2)}) async-start(), calls=%async_computation.11 | async-start | bytes 1048576 | tf_op jit(solution)/shard_map/psum | solution.py:42
Sparse Core Ops, SparseCore 0:
  9.9 36.8 all-gather.10
  49.0 63.3 all-gather.8
  118.6 62.3 all-reduce.4
  183.0 34.4 all-gather.14
  219.4 63.3 all-gather.12
  289.0 62.3 all-reduce.6
  353.5 34.4 all-gather.18
  390.1 63.3 all-gather.16
  459.7 62.3 all-reduce.8
  524.1 34.4 all-gather.22
  560.6 63.3 all-gather.20
  630.3 62.3 all-reduce.10
where the time goes:
time: 703 us; the launch traced here: 701 us
  waiting for transfers between devices  645 us (92%)
  matrix products  24.3 us (3%)
  between operations  16.2 us (2%)
  local copies, waits for them, and re-layouts  7.69 us (1%)
  other arithmetic  7.24 us (1%)
    all_gather x4, waiting for transfers between devices, layer_product(): lax.all_gather(column_part, 'col', axis=1, tiled=True)  262 us
    psum x4, waiting for transfers between devices, local(): squared = lax.psum(partial_sum, 'depth')  247 us
    all_gather x4, waiting for transfers between devices, layer_product(): inner_rows = lax.all_gather(row_part, 'row', axis=0, tiled=True)  137 us
    dot_general x4, matrix products, layer_product(): jnp.dot(lax.all_gather(column_part, 'col', axis=1, tiled=True), inner_row...  24.3 us
  transfers between devices with their start and end apart: 12, of which 12 were waited for; matrix products, arithmetic and copies ran while one was open for 1% of the time, Pallas kernels for 0%

commit v1 on v0

v1 whole, which is shorter than its diff:
```python
import jax
import jax.numpy as jnp
from jax import lax
from jax.sharding import PartitionSpec as P

TILE = 128
STEPS = 4


def exchange(parts, axis, groups=None):
    return lax.all_to_all(parts, axis, 0, 0, axis_index_groups=groups, tiled=True)


def gather(part, axis, members, groups=None):
    return exchange(jnp.broadcast_to(part[None], (members,) + part.shape), axis, groups)


def local(density, pattern, branch):
    rows, cols = lax.axis_size("row"), lax.axis_size("col")
    layers = lax.axis_size("depth")
    row, col, layer = lax.axis_index("row"), lax.axis_index("col"), lax.axis_index("depth")
    height, width = density.shape
    sub = width // layers
    core = row % 2
    cores_apart = [[x * 2 + c for x in range(rows // 2)] for c in range(2)]
    other_core = [(i, i ^ 1) for i in range(rows)]
    far = [[c + 4 * m for m in range(cols // 4)] for c in range(4)]

    row_ids = lax.broadcasted_iota(jnp.int32, pattern.shape, 0) + row * pattern.shape[0]
    col_ids = lax.broadcasted_iota(jnp.int32, pattern.shape, 1) + col * pattern.shape[1]
    tiles = jnp.where(row_ids == col_ids, 1, pattern).T.astype(jnp.float32)
    keep = jnp.repeat(jnp.repeat(tiles, TILE, axis=0), TILE, axis=1)
    keep_part = lax.dynamic_slice_in_dim(keep, layer * sub, sub, 0)

    def shifted(parts, by):
        return lax.ppermute(parts, "col", [(z, (z + by) % cols) for z in range(cols)])

    panel = density.T * keep
    part = lax.dynamic_slice_in_dim(panel, layer * sub, sub, 0)
    for step in range(STEPS):
        mine = panel.T.reshape(height // width, layers, sub, width)
        mine = lax.dynamic_index_in_dim(mine, layer, 1, keepdims=False)
        own = gather(mine, "row", rows // 2, cores_apart)
        other = lax.ppermute(own, "row", other_core)

        def product(left):
            out = jnp.dot(
                left.reshape(-1, width), panel, precision=lax.Precision.HIGH, preferred_element_type=jnp.float32
            )
            return out.reshape(rows // 2, 2, sub, height)

        both = jnp.stack([product(own), product(other)])

        def of_class(k):
            k = k % 4
            out = lax.dynamic_slice(
                both, ((k // 2) ^ core, 0, k % 2, 0, 0), (1, rows // 2, 1, sub, height)
            )
            return out.reshape(rows // 2, sub, height)

        up, down, across = of_class(col + 1), of_class(col + 3), of_class(col + 2)
        near = of_class(col)
        near = near + shifted(up, 1) + shifted(down, -1)
        near = near + jnp.concatenate([shifted(across[:2], 2), shifted(across[2:], -2)])
        squared = exchange(near, "col", far).reshape(cols // 4, sub, height).sum(0)
        part = keep_part * jnp.where(branch[step] == 1, squared, 2.0 * part - squared)
        panel = gather(part, "depth", layers).reshape(width, height)
    return panel.T


def solution(mesh):
    in_specs = (P("row", "col"), P("row", "col"), P())
    out_specs = P("row", "col")
    return jax.shard_map(local, mesh=mesh, in_specs=in_specs, out_specs=out_specs, check_vma=False)
```

time: 703 us -> 395 us (0.56)
  waiting for transfers between devices: 645 us -> 180 us
  starting transfers between devices: 0.64 us -> 101 us
  blocking collectives: 0 us -> 88.8 us
  matrix products: 24.3 us -> 5.74 us
  between operations: 16.2 us -> 3.27 us
    all_gather x8 -> x0, waiting for transfers between devices: 399 us -> none  [the longest x4 262 us: layer_product(): lax.all_gather(column_part, 'col', axis=1, tiled=True)]
    psum x4 -> x0, waiting for transfers between devices: 247 us -> none  [local(): squared = lax.psum(partial_sum, 'depth')]
    all_to_all x0 -> x4, waiting for transfers between devices: none -> 111 us  [exchange(): lax.all_to_all(parts, axis, 0, 0, axis_index_groups=groups, tiled=True)]
    all_to_all x0 -> x8, blocking collectives: none -> 88.8 us  [exchange(): lax.all_to_all(parts, axis, 0, 0, axis_index_groups=groups, tiled=True)]
    ppermute x0 -> x20, starting transfers between devices: none -> 81.6 us  [the longest x16 59.8 us: shifted(): lax.ppermute(parts, 'col', [(z, (z + by) % cols) for z in range(cols)])]
    ppermute x0 -> x20, waiting for transfers between devices: none -> 68.4 us  [the longest x16 65 us: shifted(): lax.ppermute(parts, 'col', [(z, (z + by) % cols) for z in range(cols)])]
    all_to_all x0 -> x4, starting transfers between devices: none -> 19.2 us  [exchange(): lax.all_to_all(parts, axis, 0, 0, axis_index_groups=groups, tiled=True)]
    dot_general x4 -> x8, matrix products: 24.3 us -> 5.74 us  [product(): jnp.dot(left.reshape(-1, width), panel, precision=lax.Precision.HIGH, pre...]
  transfers between devices with their start and end apart: 12 -> 24, of which waited for: 12 -> 16; matrix products, arithmetic and copies ran while one was open for 1% -> 1% of each run, Pallas kernels for 0% -> 0%
where the time goes in v1:
time: 395 us; the launch traced here: 393 us
  waiting for transfers between devices  180 us (46%)
  starting transfers between devices  101 us (26%)
  blocking collectives  88.8 us (22%)
  other arithmetic  8.7 us (2%)
  local copies, waits for them, and re-layouts  6.05 us (2%)
  matrix products  5.74 us (1%)
    all_to_all x4, waiting for transfers between devices, exchange(): lax.all_to_all(parts, axis, 0, 0, axis_index_groups=groups, tiled=True)  111 us
    all_to_all x8, blocking collectives, exchange(): lax.all_to_all(parts, axis, 0, 0, axis_index_groups=groups, tiled=True)  88.8 us
    ppermute x16, waiting for transfers between devices, shifted(): lax.ppermute(parts, 'col', [(z, (z + by) % cols) for z in range(cols)])  65 us
    ppermute x16, starting transfers between devices, shifted(): lax.ppermute(parts, 'col', [(z, (z + by) % cols) for z in range(cols)])  59.8 us
    ppermute x4, starting transfers between devices, local(): other = lax.ppermute(own, 'row', other_core)  21.8 us
    all_to_all x4, starting transfers between devices, exchange(): lax.all_to_all(parts, axis, 0, 0, axis_index_groups=groups, tiled=True)  19.2 us
  transfers between devices with their start and end apart: 24, of which 16 were waited for; matrix products, arithmetic and copies ran while one was open for 1% of the time, Pallas kernels for 0%

profile of v1, /device:TPU:1, one launch (start us, length us, event | category | flops | bytes accessed | tf_op | source)
XLA Modules:
  0.0 393.2 jit_solution(10717396529382978452)
XLA Ops:
  2.1 11.6 %all_to_all.60 = f32[4,2,64,256]{3,2,1,0:T(8,128)S(1)} all-to-all(f32[4,2,64,256]{3,2,1,0:T(8,128)S(1)} %broadcast_in_dim.70), channel_id=1, replica_groups={{0,128,256,384},{64,192,320,448},{1,129,257,385},{65,193,321,449},{2,13..., dimensions={0} | all-to-all | bytes 1048576 | tf_op jit(solution)/shard_map/all_to_all | solution.py:11
  13.6 7.7 %collective-permute-start = (f32[4,2,64,256]{3,2,1,0:T(8,128)S(1)}, f32[4,2,64,256]{3,2,1,0:T(8,128)}, u32[]{:S(2)}, u32[]{:S(2)}) collective-permute-start(f32[4,2,64,256]{3,2,1,0:T(8,128)S(1)} %all_to_all.60), channel_id=1, source_target_pairs={{0,64},{64,0},{128,192},{192,128},{256,320},{320,256},{384,448},{4... | collective-permute-start | bytes 1572872 | tf_op jit(solution)/shard_map/ppermute | solution.py:44
  27.9 8.8 %collective-permute-start.2 = (f32[4,64,512]{2,1,0:T(8,128)}, f32[4,64,512]{2,1,0:T(8,128)}, u32[]{:S(2)}, u32[]{:S(2)}) collective-permute-start(f32[4,64,512]{2,1,0:T(8,128)} %get-tuple-element.16), channel_id=1, source_target_pairs={{0,60},{4,0},{8,4},{12,8},{16,12},{20,16},{24,20},{28,24},{32,28},... | collective-permute-start | bytes 1572872 | tf_op jit(solution)/shard_map/ppermute | solution.py:36
  40.1 5.5 %collective-permute-start.4 = (f32[2,64,512]{2,1,0:T(8,128)}, f32[2,64,512]{2,1,0:T(8,128)}, u32[]{:S(2)}, u32[]{:S(2)}) collective-permute-start(f32[2,64,512]{2,1,0:T(8,128)} %slice_bitcast_fusion.6), channel_id=1, source_target_pairs={{0,56},{4,60},{8,0},{12,4},{16,8},{20,12},{24,16},{28,20},{32,24},... | collective-permute-start | bytes 786440 | tf_op jit(solution)/shard_map/ppermute | solution.py:36
  45.6 9.4 %collective-permute-done.3 = f32[2,64,512]{2,1,0:T(8,128)S(1)} collective-permute-done((f32[2,64,512]{2,1,0:T(8,128)}, f32[2,64,512]{2,1,0:T(8,128)S(1)}, u32[]{:S(2)}, u32[]{:S(2)}) %collective-permute-start.3) | collective-permute-done | bytes 262176 | tf_op jit(solution)/shard_map/ppermute | solution.py:36
  61.6 8.8 %all-to-all-start.1 = ((f32[4,64,512]{2,1,0:T(8,128)}), f32[4,64,512]{2,1,0:T(8,128)S(1)}, u32[]{:S(2)}, u32[]{:S(2)}) async-start(f32[4,64,512]{2,1,0:T(8,128)} %fusion.35), calls=%async_computation.1 | async-start | bytes 1048576 | tf_op jit(solution)/shard_map/all_to_all | solution.py:11
  71.7 26.8 %all-to-all-done.1 = f32[4,64,512]{2,1,0:T(8,128)S(1)} async-done(((f32[4,64,512]{2,1,0:T(8,128)}), f32[4,64,512]{2,1,0:T(8,128)S(1)}, u32[]{:S(2)}, u32[]{:S(2)}) %all-to-all-start.1) | async-done | bytes 524320 | tf_op jit(solution)/shard_map/all_to_all | solution.py:11
  98.6 12.5 %all_to_all.61 = f32[4,64,512]{2,1,0:T(8,128)S(1)} all-to-all(f32[4,64,512]{2,1,0:T(8,128)S(1)} %broadcast_in_dim.71), channel_id=1, replica_groups=mesh['row'=8,'col'=16,'depth'=4] {'depth'}, dimensions={0} | all-to-all | bytes 1048576 | tf_op jit(solution)/shard_map/all_to_all | solution.py:11
  111.4 9.7 %all_to_all.62 = f32[4,2,64,256]{3,2,1,0:T(8,128)S(1)} all-to-all(f32[4,2,64,256]{3,2,1,0:T(8,128)S(1)} %broadcast_in_dim.73), channel_id=1, replica_groups={{0,128,256,384},{64,192,320,448},{1,129,257,385},{65,193,321,449},{2,13..., dimensions={0} | all-to-all | bytes 1048576 | tf_op jit(solution)/shard_map/all_to_all | solution.py:11
  121.0 5.0 %collective-permute-start.5 = (f32[4,2,64,256]{3,2,1,0:T(8,128)S(1)}, f32[4,2,64,256]{3,2,1,0:T(8,128)S(1)}, u32[]{:S(2)}, u32[]{:S(2)}) collective-permute-start(f32[4,2,64,256]{3,2,1,0:T(8,128)S(1)} %all_to_all.62), channel_id=1, source_target_pairs={{0,64},{64,0},{128,192},{192,128},{256,320},{320,256},{384,448},{4... | collective-permute-start | bytes 1572872 | tf_op jit(solution)/shard_map/ppermute | solution.py:44
  142.6 8.3 %collective-permute-done.8 = f32[2,64,512]{2,1,0:T(8,128)S(1)} collective-permute-done((f32[2,64,512]{2,1,0:T(8,128)S(1)}, f32[2,64,512]{2,1,0:T(8,128)S(1)}, u32[]{:S(2)}, u32[]{:S(2)}) %collective-permute-start.8) | collective-permute-done | bytes 262176 | tf_op jit(solution)/shard_map/ppermute | solution.py:36
  150.9 9.1 %collective-permute-done.9 = f32[2,64,512]{2,1,0:T(8,128)S(1)} collective-permute-done((f32[2,64,512]{2,1,0:T(8,128)S(1)}, f32[2,64,512]{2,1,0:T(8,128)S(1)}, u32[]{:S(2)}, u32[]{:S(2)}) %collective-permute-start.9) | collective-permute-done | bytes 262176 | tf_op jit(solution)/shard_map/ppermute | solution.py:36
  165.2 28.0 %all-to-all-done.4 = f32[4,64,512]{2,1,0:T(8,128)S(1)} async-done(((f32[4,64,512]{2,1,0:T(8,128)}), f32[4,64,512]{2,1,0:T(8,128)S(1)}, u32[]{:S(2)}, u32[]{:S(2)}) %all-to-all-start.4) | async-done | bytes 524320 | tf_op jit(solution)/shard_map/all_to_all | solution.py:11
  193.4 11.5 %all_to_all.63 = f32[4,64,512]{2,1,0:T(8,128)S(1)} all-to-all(f32[4,64,512]{2,1,0:T(8,128)S(1)} %broadcast_in_dim.74), channel_id=1, replica_groups=mesh['row'=8,'col'=16,'depth'=4] {'depth'}, dimensions={0} | all-to-all | bytes 1048576 | tf_op jit(solution)/shard_map/all_to_all | solution.py:11
  205.2 10.3 %all_to_all.64 = f32[4,2,64,256]{3,2,1,0:T(8,128)S(1)} all-to-all(f32[4,2,64,256]{3,2,1,0:T(8,128)S(1)} %broadcast_in_dim.76), channel_id=1, replica_groups={{0,128,256,384},{64,192,320,448},{1,129,257,385},{65,193,321,449},{2,13..., dimensions={0} | all-to-all | bytes 1048576 | tf_op jit(solution)/shard_map/all_to_all | solution.py:11
  236.4 8.5 %collective-permute-done.13 = f32[2,64,512]{2,1,0:T(8,128)S(1)} collective-permute-done((f32[2,64,512]{2,1,0:T(8,128)S(1)}, f32[2,64,512]{2,1,0:T(8,128)S(1)}, u32[]{:S(2)}, u32[]{:S(2)}) %collective-permute-start.13) | collective-permute-done | bytes 262176 | tf_op jit(solution)/shard_map/ppermute | solution.py:36
  244.9 8.5 %collective-permute-done.14 = f32[2,64,512]{2,1,0:T(8,128)S(1)} collective-permute-done((f32[2,64,512]{2,1,0:T(8,128)S(1)}, f32[2,64,512]{2,1,0:T(8,128)S(1)}, u32[]{:S(2)}, u32[]{:S(2)}) %collective-permute-start.14) | collective-permute-done | bytes 262176 | tf_op jit(solution)/shard_map/ppermute | solution.py:36
  258.6 28.3 %all-to-all-done.7 = f32[4,64,512]{2,1,0:T(8,128)S(1)} async-done(((f32[4,64,512]{2,1,0:T(8,128)}), f32[4,64,512]{2,1,0:T(8,128)S(1)}, u32[]{:S(2)}, u32[]{:S(2)}) %all-to-all-start.7) | async-done | bytes 524320 | tf_op jit(solution)/shard_map/all_to_all | solution.py:11
  287.1 11.5 %all_to_all.65 = f32[4,64,512]{2,1,0:T(8,128)S(1)} all-to-all(f32[4,64,512]{2,1,0:T(8,128)S(1)} %broadcast_in_dim.77), channel_id=1, replica_groups=mesh['row'=8,'col'=16,'depth'=4] {'depth'}, dimensions={0} | all-to-all | bytes 1048576 | tf_op jit(solution)/shard_map/all_to_all | solution.py:11
  298.8 10.3 %all_to_all.66 = f32[4,2,64,256]{3,2,1,0:T(8,128)S(1)} all-to-all(f32[4,2,64,256]{3,2,1,0:T(8,128)S(1)} %broadcast_in_dim.79), channel_id=1, replica_groups={{0,128,256,384},{64,192,320,448},{1,129,257,385},{65,193,321,449},{2,13..., dimensions={0} | all-to-all | bytes 1048576 | tf_op jit(solution)/shard_map/all_to_all | solution.py:11
  330.1 8.5 %collective-permute-done.18 = f32[2,64,512]{2,1,0:T(8,128)S(1)} collective-permute-done((f32[2,64,512]{2,1,0:T(8,128)S(1)}, f32[2,64,512]{2,1,0:T(8,128)S(1)}, u32[]{:S(2)}, u32[]{:S(2)}) %collective-permute-start.18) | collective-permute-done | bytes 262176 | tf_op jit(solution)/shard_map/ppermute | solution.py:36
  338.5 8.5 %collective-permute-done.19 = f32[2,64,512]{2,1,0:T(8,128)S(1)} collective-permute-done((f32[2,64,512]{2,1,0:T(8,128)S(1)}, f32[2,64,512]{2,1,0:T(8,128)S(1)}, u32[]{:S(2)}, u32[]{:S(2)}) %collective-permute-start.19) | collective-permute-done | bytes 262176 | tf_op jit(solution)/shard_map/ppermute | solution.py:36
  352.2 28.4 %all-to-all-done.10 = f32[4,64,512]{2,1,0:T(8,128)S(1)} async-done(((f32[4,64,512]{2,1,0:T(8,128)}), f32[4,64,512]{2,1,0:T(8,128)S(1)}, u32[]{:S(2)}, u32[]{:S(2)}) %all-to-all-start.10) | async-done | bytes 524320 | tf_op jit(solution)/shard_map/all_to_all | solution.py:11
  380.8 11.5 %all_to_all.67 = f32[4,64,512]{2,1,0:T(8,128)S(1)} all-to-all(f32[4,64,512]{2,1,0:T(8,128)S(1)} %broadcast_in_dim.80), channel_id=1, replica_groups=mesh['row'=8,'col'=16,'depth'=4] {'depth'}, dimensions={0} | all-to-all | bytes 1048576 | tf_op jit(solution)/shard_map/all_to_all | solution.py:11
  (94 shorter events, 93.1 us)
Async XLA Ops:
  13.6 9.3 %collective-permute-start = (f32[4,2,64,256]{3,2,1,0:T(8,128)S(1)}, f32[4,2,64,256]{3,2,1,0:T(8,128)}, u32[]{:S(2)}, u32[]{:S(2)}) collective-permute-start(f32[4,2,64,256]{3,2,1,0:T(8,128)S(1)} %all_to_all.60), channel_id=1, source_target_pairs={{0,64},{64,0},{128,192},{192,128},{256,320},{320,256},{384,448},{4... | collective-permute-start | bytes 1572872 | tf_op jit(solution)/shard_map/ppermute | solution.py:44
  26.0 33.2 %collective-permute-start.1 = (f32[4,64,512]{2,1,0:T(8,128)}, f32[4,64,512]{2,1,0:T(8,128)}, u32[]{:S(2)}, u32[]{:S(2)}) collective-permute-start(f32[4,64,512]{2,1,0:T(8,128)} %get-tuple-element.15), channel_id=1, source_target_pairs={{0,4},{4,8},{8,12},{12,16},{16,20},{20,24},{24,28},{28,32},{32,36}... | collective-permute-start | bytes 1572872 | tf_op jit(solution)/shard_map/ppermute | solution.py:36
  27.9 31.3 %collective-permute-start.2 = (f32[4,64,512]{2,1,0:T(8,128)}, f32[4,64,512]{2,1,0:T(8,128)}, u32[]{:S(2)}, u32[]{:S(2)}) collective-permute-start(f32[4,64,512]{2,1,0:T(8,128)} %get-tuple-element.16), channel_id=1, source_target_pairs={{0,60},{4,0},{8,4},{12,8},{16,12},{20,16},{24,20},{28,24},{32,28},... | collective-permute-start | bytes 1572872 | tf_op jit(solution)/shard_map/ppermute | solution.py:36
  38.2 16.9 %collective-permute-start.3 = (f32[2,64,512]{2,1,0:T(8,128)}, f32[2,64,512]{2,1,0:T(8,128)S(1)}, u32[]{:S(2)}, u32[]{:S(2)}) collective-permute-start(f32[2,64,512]{2,1,0:T(8,128)} %slice_bitcast_fusion.7), channel_id=1, source_target_pairs={{0,8},{4,12},{8,16},{12,20},{16,24},{20,28},{24,32},{28,36},{32,40... | collective-permute-start | bytes 786440 | tf_op jit(solution)/shard_map/ppermute | solution.py:36
  40.1 19.1 %collective-permute-start.4 = (f32[2,64,512]{2,1,0:T(8,128)}, f32[2,64,512]{2,1,0:T(8,128)}, u32[]{:S(2)}, u32[]{:S(2)}) collective-permute-start(f32[2,64,512]{2,1,0:T(8,128)} %slice_bitcast_fusion.6), channel_id=1, source_target_pairs={{0,56},{4,60},{8,0},{12,4},{16,8},{20,12},{24,16},{28,20},{32,24},... | collective-permute-start | bytes 786440 | tf_op jit(solution)/shard_map/ppermute | solution.py:36
  61.6 36.9 %all-to-all-start.1 = ((f32[4,64,512]{2,1,0:T(8,128)}), f32[4,64,512]{2,1,0:T(8,128)S(1)}, u32[]{:S(2)}, u32[]{:S(2)}) async-start(f32[4,64,512]{2,1,0:T(8,128)} %fusion.35), calls=%async_computation.1 | async-start | bytes 1048576 | tf_op jit(solution)/shard_map/all_to_all | solution.py:11
  121.0 6.6 %collective-permute-start.5 = (f32[4,2,64,256]{3,2,1,0:T(8,128)S(1)}, f32[4,2,64,256]{3,2,1,0:T(8,128)S(1)}, u32[]{:S(2)}, u32[]{:S(2)}) collective-permute-start(f32[4,2,64,256]{3,2,1,0:T(8,128)S(1)} %all_to_all.62), channel_id=1, source_target_pairs={{0,64},{64,0},{128,192},{192,128},{256,320},{320,256},{384,448},{4... | collective-permute-start | bytes 1572872 | tf_op jit(solution)/shard_map/ppermute | solution.py:44
  128.6 31.3 %collective-permute-start.6 = (f32[4,64,512]{2,1,0:T(8,128)S(1)}, f32[4,64,512]{2,1,0:T(8,128)S(1)}, u32[]{:S(2)}, u32[]{:S(2)}) collective-permute-start(f32[4,64,512]{2,1,0:T(8,128)S(1)} %get-tuple-element.12), channel_id=1, source_target_pairs={{0,4},{4,8},{8,12},{12,16},{16,20},{20,24},{24,28},{28,32},{32,36}... | collective-permute-start | bytes 1572872 | tf_op jit(solution)/shard_map/ppermute | solution.py:36
  130.6 29.4 %collective-permute-start.7 = (f32[4,64,512]{2,1,0:T(8,128)S(1)}, f32[4,64,512]{2,1,0:T(8,128)S(1)}, u32[]{:S(2)}, u32[]{:S(2)}) collective-permute-start(f32[4,64,512]{2,1,0:T(8,128)S(1)} %get-tuple-element.13), channel_id=1, source_target_pairs={{0,60},{4,0},{8,4},{12,8},{16,12},{20,16},{24,20},{28,24},{32,28},... | collective-permute-start | bytes 1572872 | tf_op jit(solution)/shard_map/ppermute | solution.py:36
  135.2 15.7 %collective-permute-start.8 = (f32[2,64,512]{2,1,0:T(8,128)S(1)}, f32[2,64,512]{2,1,0:T(8,128)S(1)}, u32[]{:S(2)}, u32[]{:S(2)}) collective-permute-start(f32[2,64,512]{2,1,0:T(8,128)S(1)} %slice_bitcast_fusion.5), channel_id=1, source_target_pairs={{0,8},{4,12},{8,16},{12,20},{16,24},{20,28},{24,32},{28,36},{32,40... | collective-permute-start | bytes 786440 | tf_op jit(solution)/shard_map/ppermute | solution.py:36
  139.4 20.6 %collective-permute-start.9 = (f32[2,64,512]{2,1,0:T(8,128)S(1)}, f32[2,64,512]{2,1,0:T(8,128)S(1)}, u32[]{:S(2)}, u32[]{:S(2)}) collective-permute-start(f32[2,64,512]{2,1,0:T(8,128)S(1)} %slice_bitcast_fusion.4), channel_id=1, source_target_pairs={{0,56},{4,60},{8,0},{12,4},{16,8},{20,12},{24,16},{28,20},{32,24},... | collective-permute-start | bytes 786440 | tf_op jit(solution)/shard_map/ppermute | solution.py:36
  161.1 32.2 %all-to-all-start.4 = ((f32[4,64,512]{2,1,0:T(8,128)}), f32[4,64,512]{2,1,0:T(8,128)S(1)}, u32[]{:S(2)}, u32[]{:S(2)}) async-start(f32[4,64,512]{2,1,0:T(8,128)} %fusion.25), calls=%async_computation.4 | async-start | bytes 1048576 | tf_op jit(solution)/shard_map/all_to_all | solution.py:11
  215.4 6.0 %collective-permute-start.10 = (f32[4,2,64,256]{3,2,1,0:T(8,128)S(1)}, f32[4,2,64,256]{3,2,1,0:T(8,128)S(1)}, u32[]{:S(2)}, u32[]{:S(2)}) collective-permute-start(f32[4,2,64,256]{3,2,1,0:T(8,128)S(1)} %all_to_all.64), channel_id=1, source_target_pairs={{0,64},{64,0},{128,192},{192,128},{256,320},{320,256},{384,448},{4... | collective-permute-start | bytes 1572872 | tf_op jit(solution)/shard_map/ppermute | solution.py:44
  222.4 31.0 %collective-permute-start.11 = (f32[4,64,512]{2,1,0:T(8,128)S(1)}, f32[4,64,512]{2,1,0:T(8,128)S(1)}, u32[]{:S(2)}, u32[]{:S(2)}) collective-permute-start(f32[4,64,512]{2,1,0:T(8,128)S(1)} %get-tuple-element.9), channel_id=1, source_target_pairs={{0,4},{4,8},{8,12},{12,16},{16,20},{20,24},{24,28},{28,32},{32,36}... | collective-permute-start | bytes 1572872 | tf_op jit(solution)/shard_map/ppermute | solution.py:36
  224.4 29.1 %collective-permute-start.12 = (f32[4,64,512]{2,1,0:T(8,128)S(1)}, f32[4,64,512]{2,1,0:T(8,128)S(1)}, u32[]{:S(2)}, u32[]{:S(2)}) collective-permute-start(f32[4,64,512]{2,1,0:T(8,128)S(1)} %get-tuple-element.10), channel_id=1, source_target_pairs={{0,60},{4,0},{8,4},{12,8},{16,12},{20,16},{24,20},{28,24},{32,28},... | collective-permute-start | bytes 1572872 | tf_op jit(solution)/shard_map/ppermute | solution.py:36
  229.0 15.9 %collective-permute-start.13 = (f32[2,64,512]{2,1,0:T(8,128)S(1)}, f32[2,64,512]{2,1,0:T(8,128)S(1)}, u32[]{:S(2)}, u32[]{:S(2)}) collective-permute-start(f32[2,64,512]{2,1,0:T(8,128)S(1)} %slice_bitcast_fusion.3), channel_id=1, source_target_pairs={{0,8},{4,12},{8,16},{12,20},{16,24},{20,28},{24,32},{28,36},{32,40... | collective-permute-start | bytes 786440 | tf_op jit(solution)/shard_map/ppermute | solution.py:36
  232.8 20.6 %collective-permute-start.14 = (f32[2,64,512]{2,1,0:T(8,128)S(1)}, f32[2,64,512]{2,1,0:T(8,128)S(1)}, u32[]{:S(2)}, u32[]{:S(2)}) collective-permute-start(f32[2,64,512]{2,1,0:T(8,128)S(1)} %slice_bitcast_fusion.2), channel_id=1, source_target_pairs={{0,56},{4,60},{8,0},{12,4},{16,8},{20,12},{24,16},{28,20},{32,24},... | collective-permute-start | bytes 786440 | tf_op jit(solution)/shard_map/ppermute | solution.py:36
  254.5 32.4 %all-to-all-start.7 = ((f32[4,64,512]{2,1,0:T(8,128)}), f32[4,64,512]{2,1,0:T(8,128)S(1)}, u32[]{:S(2)}, u32[]{:S(2)}) async-start(f32[4,64,512]{2,1,0:T(8,128)} %fusion.15), calls=%async_computation.7 | async-start | bytes 1048576 | tf_op jit(solution)/shard_map/all_to_all | solution.py:11
  309.1 6.0 %collective-permute-start.15 = (f32[4,2,64,256]{3,2,1,0:T(8,128)S(1)}, f32[4,2,64,256]{3,2,1,0:T(8,128)S(1)}, u32[]{:S(2)}, u32[]{:S(2)}) collective-permute-start(f32[4,2,64,256]{3,2,1,0:T(8,128)S(1)} %all_to_all.66), channel_id=1, source_target_pairs={{0,64},{64,0},{128,192},{192,128},{256,320},{320,256},{384,448},{4... | collective-permute-start | bytes 1572872 | tf_op jit(solution)/shard_map/ppermute | solution.py:44
  316.1 31.0 %collective-permute-start.16 = (f32[4,64,512]{2,1,0:T(8,128)S(1)}, f32[4,64,512]{2,1,0:T(8,128)S(1)}, u32[]{:S(2)}, u32[]{:S(2)}) collective-permute-start(f32[4,64,512]{2,1,0:T(8,128)S(1)} %get-tuple-element.6), channel_id=1, source_target_pairs={{0,4},{4,8},{8,12},{12,16},{16,20},{20,24},{24,28},{28,32},{32,36}... | collective-permute-start | bytes 1572872 | tf_op jit(solution)/shard_map/ppermute | solution.py:36
  318.0 29.0 %collective-permute-start.17 = (f32[4,64,512]{2,1,0:T(8,128)S(1)}, f32[4,64,512]{2,1,0:T(8,128)S(1)}, u32[]{:S(2)}, u32[]{:S(2)}) collective-permute-start(f32[4,64,512]{2,1,0:T(8,128)S(1)} %get-tuple-element.7), channel_id=1, source_target_pairs={{0,60},{4,0},{8,4},{12,8},{16,12},{20,16},{24,20},{28,24},{32,28},... | collective-permute-start | bytes 1572872 | tf_op jit(solution)/shard_map/ppermute | solution.py:36
  322.6 15.9 %collective-permute-start.18 = (f32[2,64,512]{2,1,0:T(8,128)S(1)}, f32[2,64,512]{2,1,0:T(8,128)S(1)}, u32[]{:S(2)}, u32[]{:S(2)}) collective-permute-start(f32[2,64,512]{2,1,0:T(8,128)S(1)} %slice_bitcast_fusion.1), channel_id=1, source_target_pairs={{0,8},{4,12},{8,16},{12,20},{16,24},{20,28},{24,32},{28,36},{32,40... | collective-permute-start | bytes 786440 | tf_op jit(solution)/shard_map/ppermute | solution.py:36
  326.4 20.6 %collective-permute-start.19 = (f32[2,64,512]{2,1,0:T(8,128)S(1)}, f32[2,64,512]{2,1,0:T(8,128)S(1)}, u32[]{:S(2)}, u32[]{:S(2)}) collective-permute-start(f32[2,64,512]{2,1,0:T(8,128)S(1)} %slice_bitcast_fusion), channel_id=1, source_target_pairs={{0,56},{4,60},{8,0},{12,4},{16,8},{20,12},{24,16},{28,20},{32,24},... | collective-permute-start | bytes 786440 | tf_op jit(solution)/shard_map/ppermute | solution.py:36
  348.1 32.5 %all-to-all-start.10 = ((f32[4,64,512]{2,1,0:T(8,128)}), f32[4,64,512]{2,1,0:T(8,128)S(1)}, u32[]{:S(2)}, u32[]{:S(2)}) async-start(f32[4,64,512]{2,1,0:T(8,128)} %fusion.5), calls=%async_computation.10 | async-start | bytes 1048576 | tf_op jit(solution)/shard_map/all_to_all | solution.py:11
  (2 other events, 10.1 us)

commit v2 on v1

v2 whole, which is shorter than its diff:
```python
import functools

import jax
import jax.numpy as jnp
from jax import lax
from jax.experimental import pallas as pl
from jax.experimental.pallas import tpu as pltpu
from jax.sharding import PartitionSpec as P

TILE = 128
STEPS = 4
LANES = 8
NATURAL = 18
BALANCED = 14


def exchange(parts, axis, groups=None):
    return lax.all_to_all(parts, axis, 0, 0, axis_index_groups=groups, tiled=True)


def gather(part, axis, members, groups=None):
    return exchange(jnp.broadcast_to(part[None], (members,) + part.shape), axis, groups)


def shifted(parts, by):
    cols = lax.axis_size("col")
    return lax.ppermute(parts, "col", [(z, (z + by) % cols) for z in range(cols)])


def sum_along_col(ahead):
    cols = lax.axis_size("col")
    far = [[c + 4 * m for m in range(cols // 4)] for c in range(4)]
    near = ahead[0] + shifted(ahead[1], 1) + shifted(ahead[3], -1)
    near = near + jnp.concatenate([shifted(ahead[2][:2], 2), shifted(ahead[2][2:], -2)])
    return exchange(near, "col", far).sum(0)


def swap_cores(value):
    return lax.ppermute(value, "row", [(i, i ^ 1) for i in range(lax.axis_size("row"))])


def dense(density, pattern, branch):
    rows, cols = lax.axis_size("row"), lax.axis_size("col")
    layers = lax.axis_size("depth")
    row, col, layer = lax.axis_index("row"), lax.axis_index("col"), lax.axis_index("depth")
    height, width = density.shape
    sub = width // layers
    core = row % 2
    cores_apart = [[x * 2 + c for x in range(rows // 2)] for c in range(2)]

    row_ids = lax.broadcasted_iota(jnp.int32, pattern.shape, 0) + row * pattern.shape[0]
    col_ids = lax.broadcasted_iota(jnp.int32, pattern.shape, 1) + col * pattern.shape[1]
    tiles = jnp.where(row_ids == col_ids, 1, pattern).T.astype(jnp.float32)
    keep = jnp.repeat(jnp.repeat(tiles, TILE, axis=0), TILE, axis=1)
    keep_part = lax.dynamic_slice_in_dim(keep, layer * sub, sub, 0)

    panel = density.T * keep
    part = lax.dynamic_slice_in_dim(panel, layer * sub, sub, 0)
    for step in range(STEPS):
        mine = panel.T.reshape(height // width, layers, sub, width)
        mine = lax.dynamic_index_in_dim(mine, layer, 1, keepdims=False)
        own = gather(mine, "row", rows // 2, cores_apart)
        other = swap_cores(own)

        def product(left, panel=panel):
            out = jnp.dot(
                left.reshape(-1, width), panel, precision=lax.Precision.HIGH, preferred_element_type=jnp.float32
            )
            return out.reshape(rows // 2, 2, sub, height)

        both = jnp.stack([product(own), product(other)])

        def of_class(k, both=both):
            k = k % 4
            start = ((k // 2) ^ core, 0, k % 2, 0, 0)
            out = lax.dynamic_slice(both, start, (1, rows // 2, 1, sub, height))
            return out.reshape(rows // 2, sub, height)

        squared = sum_along_col([of_class(col + q) for q in range(4)])
        part = keep_part * jnp.where(branch[step] == 1, squared, 2.0 * part - squared)
        panel = gather(part, "depth", layers).reshape(width, height)
    return panel.T


def column_order(keep):
    n = keep.shape[0]
    load = keep.sum(0)
    ids = jnp.arange(n)
    ahead = (load[None, :] > load[:, None]) | ((load[None, :] == load[:, None]) & (ids[None, :] < ids[:, None]))
    rank = ahead.astype(jnp.int32).sum(1)
    place = jnp.where(rank < n // 2, 2 * rank, 2 * (n - 1 - rank) + 1)
    return jnp.where(place[None, :] == ids[:, None], ids[None, :], 0).sum(1)


def slot_lists(keep, order, slots):
    n = keep.shape[0]
    ids = jnp.arange(n)
    held = ((order[:, None] == ids[None, :])[:, :, None] & (keep[None, :, :] > 0)).any(1)
    held = held.reshape(n // 2, 2 * n)
    count = jnp.cumsum(held.astype(jnp.int32), axis=1)
    which = held[:, :, None] & (count[:, :, None] - 1 == jnp.arange(2 * slots)[None, None, :])
    spots = jnp.arange(2 * n)
    there = which.any(1)
    code = jnp.where(which, spots[None, :, None], 0).sum(1)
    source = order.reshape(n // 2, 2)[:, spots // n] * n + (spots % n)[None, :]
    source = jnp.where(which, source[:, :, None], 0).sum(1)
    return jnp.where(there, code, -1), jnp.where(there, source, -1), count[:, -1].max()


def pick_kernel(info_ref, from_ref, out_ref, *, slots, blocks):
    for t in range(slots):
        code = info_ref[t]
        at = jnp.maximum(code, 0)
        rows = pl.ds(pl.multiple_of((at // blocks) * LANES, LANES), LANES)
        lanes = pl.ds(pl.multiple_of((at % blocks) * TILE, TILE), TILE)
        out_ref[t * LANES : (t + 1) * LANES, :] = jnp.where(code >= 0, from_ref[rows, lanes], 0.0)


def place_kernel(info_ref, own_ref, other_ref, out_ref, *, slots, blocks):
    out_ref[...] = jnp.zeros_like(out_ref)
    for base, ref in ((0, own_ref), (slots, other_ref)):
        for t in range(slots):
            code = info_ref[base + t]

            @pl.when(code >= 0)
            def _(code=code, ref=ref, t=t):
                rows = pl.ds(pl.multiple_of((code // blocks) * LANES, LANES), LANES)
                lanes = pl.ds(pl.multiple_of((code % blocks) * TILE, TILE), TILE)
                out_ref[rows, lanes] = ref[t * LANES : (t + 1) * LANES, :]


def step_kernel(info_ref, own_ref, other_ref, out_ref, x_ref, hi_ref, lo_ref, left_hi, left_lo, prod_ref,
                *, slots_in, slots_out, blocks):
    share, square = info_ref[0], info_ref[3]
    sharers = TILE // LANES
    x_ref[...] = jnp.zeros_like(x_ref)
    for base, ref in ((4, own_ref), (4 + slots_in, other_ref)):

        def place(t, _, base=base, ref=ref):
            code = info_ref[base + t]

            @pl.when(code >= 0)
            def _():
                lanes = pl.ds(pl.multiple_of((code % blocks) * TILE, TILE), TILE)
                rows = pl.ds(pl.multiple_of(t * LANES, LANES), LANES)
                for s in range(sharers):
                    at = pl.multiple_of((code // blocks) * TILE + s * LANES, LANES)
                    x_ref[pl.ds(at, LANES), lanes] = ref[s, rows, :]

            return 0

        lax.fori_loop(0, slots_in, place, 0)

    one = lax.broadcasted_iota(jnp.int32, (LANES, TILE), 1) == share * LANES + lax.broadcasted_iota(
        jnp.int32, (LANES, TILE), 0
    )
    one = jnp.where(one, 1.0, 0.0).astype(jnp.bfloat16)
    across = (((1,), (1,)), ((), ()))
    for j in range(blocks):
        lanes = slice(j * TILE, (j + 1) * TILE)
        x = x_ref[:, lanes]
        hi = x.astype(jnp.bfloat16)
        lo = (x - hi.astype(jnp.float32)).astype(jnp.bfloat16)
        hi_ref[:, lanes] = hi
        lo_ref[:, lanes] = lo
        rows = slice(j * LANES, (j + 1) * LANES)
        left_hi[rows, :] = lax.dot_general(one, hi, across, preferred_element_type=jnp.float32)
        left_lo[rows, :] = lax.dot_general(one, lo, across, preferred_element_type=jnp.float32)
    a_hi = left_hi[...].astype(jnp.bfloat16)
    a_lo = left_lo[...].astype(jnp.bfloat16)
    wide = 4 * TILE
    for j in range(blocks * TILE // wide):
        lanes = slice(j * wide, (j + 1) * wide)
        b_hi, b_lo = hi_ref[:, lanes], lo_ref[:, lanes]
        prod_ref[:, lanes] = (
            jnp.dot(a_hi, b_hi, preferred_element_type=jnp.float32)
            + jnp.dot(a_hi, b_lo, preferred_element_type=jnp.float32)
            + jnp.dot(a_lo, b_hi, preferred_element_type=jnp.float32)
        )

    sign = jnp.where(square == 1, 1.0, -1.0)
    weight = jnp.where(square == 1, 0.0, -2.0)
    for half in range(2):
        rows = pl.ds(pl.multiple_of(info_ref[1 + half] * LANES, LANES), LANES)
        mine = pl.ds(pl.multiple_of(half * TILE + share * LANES, LANES), LANES)
        prod_ref[rows, :] = prod_ref[rows, :] + weight * x_ref[mine, :]

    first = 4 + 2 * slots_in

    def pick(t, _):
        code = info_ref[first + t]
        at = jnp.maximum(code, 0)
        rows = pl.ds(pl.multiple_of((at // blocks) * LANES, LANES), LANES)
        lanes = pl.ds(pl.multiple_of((at % blocks) * TILE, TILE), TILE)
        out = pl.ds(pl.multiple_of(t * LANES, LANES), LANES)
        out_ref[out, :] = jnp.where(code >= 0, sign * prod_ref[rows, lanes], 0.0)
        return 0

    lax.fori_loop(0, out_ref.shape[0] // LANES, pick, 0, unroll=8)


def on_core(kernel, shape, scratch=(), vmem=None):
    vmem_spec, smem_spec = pl.BlockSpec(memory_space=pltpu.VMEM), pl.BlockSpec(memory_space=pltpu.SMEM)

    def call(info, *arrays):
        return pl.pallas_call(
            kernel,
            out_shape=jax.ShapeDtypeStruct(shape, jnp.float32),
            in_specs=[smem_spec] + [vmem_spec] * len(arrays),
            out_specs=vmem_spec,
            scratch_shapes=list(scratch),
            compiler_params=pltpu.CompilerParams(vmem_limit_bytes=vmem),
        )(info, *arrays)

    return call


def sparse(strips, keep, lists, branch):
    rows, cols, layers = lax.axis_size("row"), lax.axis_size("col"), lax.axis_size("depth")
    row, col, layer = lax.axis_index("row"), lax.axis_index("col"), lax.axis_index("depth")
    core, share = row % 2, (row // 2) * layers + layer
    sharers, blocks = TILE // LANES, keep.shape[0]
    order = blocks * TILE
    in_plane = [
        [(x * 2 + c) * layers + y for x in range(rows // 2) for y in range(layers)] for c in range(2)
    ]
    bytes_limit = 48 * 1024 * 1024

    def of_plane(which, core):
        codes = lists[which][1].reshape(cols, 2, -1)
        return lax.dynamic_slice(codes, (col, core, 0), (1, 1, codes.shape[2])).reshape(-1)

    def for_planes(which):
        sources = lists[which][2].reshape(cols // 4, 4, 2, -1)
        sources = lax.dynamic_index_in_dim(sources, core, 2, keepdims=False)
        twice = jnp.concatenate([sources, sources], axis=1)
        return lax.dynamic_slice_in_dim(twice, col % 4, 4, 1).transpose(1, 0, 2).reshape(-1)

    natural = of_plane("natural", core)
    part = on_core(
        functools.partial(pick_kernel, slots=NATURAL, blocks=blocks), (NATURAL * LANES, TILE), vmem=bytes_limit
    )(natural, strips)
    layouts = ["natural"] + ["balanced"] * (STEPS - 1) + ["natural"]
    size = {"natural": NATURAL, "balanced": BALANCED}
    for step in range(STEPS):
        now, then = layouts[step], layouts[step + 1]
        own = gather(part, ("row", "depth"), sharers, in_plane)
        other = swap_cores(own)
        held = lax.dynamic_slice_in_dim(lists[now][0], 2 * col, 2, 0)
        info = jnp.concatenate(
            [share[None], held, branch[step][None], of_plane(now, core), of_plane(now, 1 - core), for_planes(then)]
        ).astype(jnp.int32)
        wide = 2 * TILE
        out = on_core(
            functools.partial(step_kernel, slots_in=size[now], slots_out=size[then], blocks=blocks),
            (cols * size[then] * LANES, TILE),
            scratch=(
                pltpu.VMEM((wide, order), jnp.float32),
                pltpu.VMEM((wide, order), jnp.bfloat16),
                pltpu.VMEM((wide, order), jnp.bfloat16),
                pltpu.VMEM((blocks * LANES, wide), jnp.float32),
                pltpu.VMEM((blocks * LANES, wide), jnp.float32),
                pltpu.VMEM((blocks * LANES, order), jnp.float32),
            ),
            vmem=bytes_limit,
        )(info, own, other)
        part = sum_along_col(out.reshape(4, cols // 4, size[then] * LANES, TILE))

    info = jnp.concatenate([natural, of_plane("natural", 1 - core)])
    strips = on_core(
        functools.partial(place_kernel, slots=NATURAL, blocks=blocks), strips.shape, vmem=bytes_limit
    )(info, part, swap_cores(part))
    height = order // rows
    cut = strips.reshape(2 * LANES, rows // 2, 2, height)
    cut = lax.dynamic_index_in_dim(cut, core, 2, keepdims=False).transpose(1, 0, 2)
    cut = jnp.broadcast_to(cut[:, None], (rows // 2, layers) + cut.shape[1:]).reshape(sharers, 2 * LANES, height)
    back = exchange(cut, ("row", "depth"), in_plane)
    back = back.reshape(sharers, 2, LANES, height).transpose(1, 0, 2, 3).reshape(2 * TILE, height)
    return back.T


def local(density, pattern, branch):
    rows, cols, layers = lax.axis_size("row"), lax.axis_size("col"), lax.axis_size("depth")
    layer = lax.axis_index("depth")
    height, width = density.shape
    blocks = rows * pattern.shape[0]
    cut = density.T.reshape(2, rows // 2, layers, LANES, height)
    cut = lax.dynamic_index_in_dim(cut, layer, 2, keepdims=False).transpose(1, 0, 2, 3)
    cut = cut.reshape(rows // 2, 2 * LANES, height)
    marks = jnp.zeros((LANES, height), jnp.float32).at[:2, : pattern.shape[0]].set(pattern.T.astype(jnp.float32))
    cut = jnp.concatenate([cut, jnp.broadcast_to(marks[None], (rows // 2,) + marks.shape)], axis=1)
    cut = jnp.broadcast_to(cut[:, None], (rows // 2, 2) + cut.shape[1:]).reshape((rows,) + cut.shape[1:])
    got = exchange(cut, "row")
    strips = got[:, : 2 * LANES].transpose(1, 0, 2).reshape(2 * LANES, rows * height)
    marks = got[:, 2 * LANES : 2 * LANES + 2, : pattern.shape[0]].transpose(1, 0, 2).reshape(2, blocks)
    marks = jnp.zeros((LANES, TILE), jnp.float32).at[:2, :blocks].set(marks)
    marks = gather(marks, "col", cols)[:, :2, :blocks].reshape(blocks, blocks)
    ids = jnp.arange(blocks)
    keep = jnp.where(ids[:, None] == ids[None, :], 1, marks.astype(jnp.int32))
    lists, fits = {}, True
    for name, order, slots in (("natural", ids, NATURAL), ("balanced", column_order(keep), BALANCED)):
        code, source, most = slot_lists(keep, order, slots)
        lists[name] = (order, code, source)
        fits = fits & (most <= 2 * slots)
    return lax.cond(
        fits,
        lambda: sparse(strips, keep, lists, branch),
        lambda: dense(density, pattern, branch),
    )


def solution(mesh):
    in_specs = (P("row", "col"), P("row", "col"), P())
    out_specs = P("row", "col")
    return jax.shard_map(local, mesh=mesh, in_specs=in_specs, out_specs=out_specs, check_vma=False)
```

time: 395 us -> 375 us (0.949)
  waiting for transfers between devices: 180 us -> 48 us
  blocking collectives: 88.8 us -> 150 us
  Pallas kernels: 0 us -> 29.6 us
  starting transfers between devices: 101 us -> 119 us
  local copies, waits for them, and re-layouts: 6.05 us -> 14 us
  matrix products: 5.74 us -> 0 us
    all_to_all x4 -> x2, waiting for transfers between devices: 111 us -> 19.6 us  [exchange(): lax.all_to_all(parts, axis, 0, 0, axis_index_groups=groups, tiled=True)]
    all_to_all x8 -> x9, blocking collectives: 88.8 us -> 150 us  [exchange(): lax.all_to_all(parts, axis, 0, 0, axis_index_groups=groups, tiled=True)]
    ppermute x16, waiting for transfers between devices: 65 us -> 24.2 us  [shifted(): lax.ppermute(parts, 'col', [(z, (z + by) % cols) for z in range(cols)])]
    pallas_call x0 -> x6, Pallas kernels: none -> 29.6 us  [call(): pl.pallas_call(kernel, out_shape=jax.ShapeDtypeStruct(shape, jnp.float32)...]
    ppermute x4 -> x5, starting transfers between devices: 21.8 us -> 38.2 us  [swap_cores(): lax.ppermute(value, 'row', [(i, i ^ 1) for i in range(lax.axis_size('row'...]
    dot_general x8 -> x0, matrix products: 5.74 us -> none  [product(): jnp.dot(left.reshape(-1, width), panel, precision=lax.Precision.HIGH, pre...]
    add x6, other arithmetic: 5.63 us -> 0.34 us  [the longest x4 0.19 us: sum_along_col(): near + jnp.concatenate([shifted(ahead[2][:2], 2), shifted(ahead[2][2:], -...]
    all_to_all x4 -> x2, starting transfers between devices: 19.2 us -> 20.8 us  [exchange(): lax.all_to_all(parts, axis, 0, 0, axis_index_groups=groups, tiled=True)]
  transfers between devices with their start and end apart: 24 -> 23, of which waited for: 16 -> 14; matrix products, arithmetic and copies ran while one was open for 1% -> 2% of each run, Pallas kernels for 0% -> 0%
where the time goes in v2:
time: 375 us; the launch traced here: 371 us
  blocking collectives  150 us (40%)
  starting transfers between devices  119 us (32%)
  waiting for transfers between devices  48 us (13%)
  Pallas kernels  29.6 us (8%)
  local copies, waits for them, and re-layouts  14 us (4%)
  other arithmetic  7.43 us (2%)
    all_to_all x9, blocking collectives, exchange(): lax.all_to_all(parts, axis, 0, 0, axis_index_groups=groups, tiled=True)  150 us
    ppermute x16, starting transfers between devices, shifted(): lax.ppermute(parts, 'col', [(z, (z + by) % cols) for z in range(cols)])  60.4 us
    ppermute x5, starting transfers between devices, swap_cores(): lax.ppermute(value, 'row', [(i, i ^ 1) for i in range(lax.axis_size('row'...  38.2 us
    pallas_call x6, Pallas kernels, call(): pl.pallas_call(kernel, out_shape=jax.ShapeDtypeStruct(shape, jnp.float32)...  29.6 us
    ppermute x16, waiting for transfers between devices, shifted(): lax.ppermute(parts, 'col', [(z, (z + by) % cols) for z in range(cols)])  24.2 us
    all_to_all x2, starting transfers between devices, exchange(): lax.all_to_all(parts, axis, 0, 0, axis_index_groups=groups, tiled=True)  20.8 us
    all_to_all x2, waiting for transfers between devices, exchange(): lax.all_to_all(parts, axis, 0, 0, axis_index_groups=groups, tiled=True)  19.6 us
  transfers between devices with their start and end apart: 23, of which 14 were waited for; matrix products, arithmetic and copies ran while one was open for 2% of the time, Pallas kernels for 0%

profile of v2, /device:TPU:1, one launch (start us, length us, event | category | flops | bytes accessed | tf_op | source)
XLA Modules:
  0.0 370.7 jit_solution(17060272454677838464)
XLA Ops:
  2.8 10.2 %all-to-all-start.21 = ((f32[8,24,512]{2,1,0:T(8,128)}), f32[8,24,512]{2,1,0:T(8,128)S(1)}, u32[]{:S(2)}, u32[]{:S(2)}) async-start(f32[8,24,512]{2,1,0:T(8,128)} %bitcast.117), calls=%async_computation.21 | async-start | bytes 786432 | tf_op jit(solution)/shard_map/all_to_all | solution.py:18
  13.0 8.1 %all-to-all-done.21 = f32[8,24,512]{2,1,0:T(8,128)S(1)} async-done(((f32[8,24,512]{2,1,0:T(8,128)}), f32[8,24,512]{2,1,0:T(8,128)S(1)}, u32[]{:S(2)}, u32[]{:S(2)}) %all-to-all-start.21) | async-done | bytes 393248 | tf_op jit(solution)/shard_map/all_to_all | solution.py:18
  21.9 10.6 %all-to-all-start.22 = ((f32[16,8,128]{2,1,0:T(8,128)}), f32[16,8,128]{2,1,0:T(8,128)S(1)}, u32[]{:S(2)}, u32[]{:S(2)}) async-start(f32[16,8,128]{2,1,0:T(8,128)} %broadcast_in_dim.166), calls=%async_computation.22 | async-start | bytes 131072 | tf_op jit(solution)/shard_map/all_to_all | solution.py:18
  32.5 11.6 %all-to-all-done.22 = f32[16,8,128]{2,1,0:T(8,128)S(1)} async-done(((f32[16,8,128]{2,1,0:T(8,128)}), f32[16,8,128]{2,1,0:T(8,128)S(1)}, u32[]{:S(2)}, u32[]{:S(2)}) %all-to-all-start.22) | async-done | bytes 65568 | tf_op jit(solution)/shard_map/all_to_all | solution.py:18
  51.6 318.3 %conditional.1 = (f32[512,256]{1,0:T(8,128)S(1)}) conditional(s32[]{:T(128)} %convert_element_type.42, (s32[4,2]{0,1:T(2,128)S(1)}, s32[4]{0:T(128)S(1)}, f32[512,256]{1,0:T(8,128)S(1)}) %tuple.140, (pred[16,64]{1,0:T(8,128)(4,1)S(1)}, s32[16,64]{1,0:T(8,128)S(1)}, s32[16,64,36]{2,1,0:T(8,128)}, s32[16,64,36]{2,1,0:T(8,128)}, s32[32]{0:T(128)S(1)}, ...), branch_computations={%region_9.14_spmd, %region_14.25_spmd} | conditional | flops 3226468352 | bytes 121121880 | solution.py:305
  55.3 20.4 %all_to_all.102.own_ref = f32[16,144,128]{2,1,0:T(8,128)S(1)} all-to-all(f32[16,144,128]{2,1,0:T(8,128)S(1)} %broadcast_in_dim.115), channel_id=1, replica_groups={{0,1,2,3,128,129,130,131,256,257,258,259,384,385,386,387},{64,65,66,67,..., dimensions={0} | all-to-all | bytes 2359296 | tf_op jit(solution)/shard_map/cond/branch_1_fun/all_to_all | solution.py:18
  85.7 6.9 %branch_1_fun.7 = f32[1792,128]{1,0:T(8,128)S(1)} custom-call(s32[264]{0:T(512)S(1)} %concatenate.48.info_ref, f32[16,144,128]{2,1,0:T(8,128)S(1)} %all_to_all.102.own_ref, f32[16,144,128]{2,1,0:T(8,128)S(1)} %collective-permute-done.other_ref), custom_call_target="tpu_custom_call" | custom-call | tf_op jit(solution)/shard_map/cond/branch_1_fun/pallas_call | solution.py:206
  111.3 19.4 %all_to_all.103 = f32[4,112,128]{2,1,0:T(8,128)S(1)} all-to-all(f32[4,112,128]{2,1,0:T(8,128)S(1)} %maximum_add_fusion.1), channel_id=1, replica_groups={{0,16,32,48},{4,20,36,52},{8,24,40,56},{12,28,44,60},{1,17,33,49},{5,21..., dimensions={0} | all-to-all | bytes 458752 | tf_op jit(solution)/shard_map/cond/branch_1_fun/all_to_all | solution.py:18
  130.8 14.1 %all_to_all.104.own_ref = f32[16,112,128]{2,1,0:T(8,128)S(1)} all-to-all(f32[16,112,128]{2,1,0:T(8,128)S(1)} %broadcast_in_dim.116), channel_id=1, replica_groups={{0,1,2,3,128,129,130,131,256,257,258,259,384,385,386,387},{64,65,66,67,..., dimensions={0} | all-to-all | bytes 1835008 | tf_op jit(solution)/shard_map/cond/branch_1_fun/all_to_all | solution.py:18
  144.9 7.5 %collective-permute-start.5 = (f32[16,112,128]{2,1,0:T(8,128)S(1)}, f32[16,112,128]{2,1,0:T(8,128)S(1)}, u32[]{:S(2)}, u32[]{:S(2)}) collective-permute-start(f32[16,112,128]{2,1,0:T(8,128)S(1)} %all_to_all.104.own_ref), channel_id=1, source_target_pairs={{0,64},{64,0},{128,192},{192,128},{256,320},{320,256},{384,448},{4... | collective-permute-start | bytes 2752520 | tf_op jit(solution)/shard_map/cond/branch_1_fun/ppermute | solution.py:39
  154.5 6.8 %branch_1_fun.8 = f32[1792,128]{1,0:T(8,128)S(1)} custom-call(s32[256]{0:T(256)S(1)} %concatenate.47.info_ref, f32[16,112,128]{2,1,0:T(8,128)S(1)} %all_to_all.104.own_ref, f32[16,112,128]{2,1,0:T(8,128)S(1)} %collective-permute-done.5.other_ref), custom_call_target="tpu_custom_call" | custom-call | tf_op jit(solution)/shard_map/cond/branch_1_fun/pallas_call | solution.py:206
  167.9 6.5 %collective-permute-start.8 = (f32[2,112,128]{2,1,0:T(8,128)S(1)}, f32[2,112,128]{2,1,0:T(8,128)S(1)}, u32[]{:S(2)}, u32[]{:S(2)}) collective-permute-start(f32[2,112,128]{2,1,0:T(8,128)S(1)} %bitcast.283), channel_id=1, source_target_pairs={{0,8},{4,12},{8,16},{12,20},{16,24},{20,28},{24,32},{28,36},{32,40... | collective-permute-start | bytes 344072 | tf_op jit(solution)/shard_map/cond/branch_1_fun/ppermute | solution.py:27
  178.4 6.0 %collective-permute-done.9 = f32[2,112,128]{2,1,0:T(8,128)S(1)} collective-permute-done((f32[2,112,128]{2,1,0:T(8,128)S(1)}, f32[2,112,128]{2,1,0:T(8,128)S(1)}, u32[]{:S(2)}, u32[]{:S(2)}) %collective-permute-start.9) | collective-permute-done | bytes 114720 | tf_op jit(solution)/shard_map/cond/branch_1_fun/ppermute | solution.py:27
  184.4 16.1 %all_to_all.105 = f32[4,112,128]{2,1,0:T(8,128)S(1)} all-to-all(f32[4,112,128]{2,1,0:T(8,128)S(1)} %maximum_add_fusion.2), channel_id=1, replica_groups={{0,16,32,48},{4,20,36,52},{8,24,40,56},{12,28,44,60},{1,17,33,49},{5,21..., dimensions={0} | all-to-all | bytes 458752 | tf_op jit(solution)/shard_map/cond/branch_1_fun/all_to_all | solution.py:18
  200.6 13.9 %all_to_all.106.own_ref = f32[16,112,128]{2,1,0:T(8,128)S(1)} all-to-all(f32[16,112,128]{2,1,0:T(8,128)S(1)} %broadcast_in_dim.117), channel_id=1, replica_groups={{0,1,2,3,128,129,130,131,256,257,258,259,384,385,386,387},{64,65,66,67,..., dimensions={0} | all-to-all | bytes 1835008 | tf_op jit(solution)/shard_map/cond/branch_1_fun/all_to_all | solution.py:18
  214.5 10.0 %collective-permute-start.10 = (f32[16,112,128]{2,1,0:T(8,128)S(1)}, f32[16,112,128]{2,1,0:T(8,128)S(1)}, u32[]{:S(2)}, u32[]{:S(2)}) collective-permute-start(f32[16,112,128]{2,1,0:T(8,128)S(1)} %all_to_all.106.own_ref), channel_id=1, source_target_pairs={{0,64},{64,0},{128,192},{192,128},{256,320},{320,256},{384,448},{4... | collective-permute-start | bytes 2752520 | tf_op jit(solution)/shard_map/cond/branch_1_fun/ppermute | solution.py:39
  226.3 6.8 %branch_1_fun.9 = f32[1792,128]{1,0:T(8,128)S(1)} custom-call(s32[256]{0:T(256)S(1)} %concatenate.46.info_ref, f32[16,112,128]{2,1,0:T(8,128)S(1)} %all_to_all.106.own_ref, f32[16,112,128]{2,1,0:T(8,128)S(1)} %collective-permute-done.10.other_ref), custom_call_target="tpu_custom_call" | custom-call | tf_op jit(solution)/shard_map/cond/branch_1_fun/pallas_call | solution.py:206
  237.4 6.1 %collective-permute-start.12 = (f32[4,112,128]{2,1,0:T(8,128)S(1)}, f32[4,112,128]{2,1,0:T(8,128)S(1)}, u32[]{:S(2)}, u32[]{:S(2)}) collective-permute-start(f32[4,112,128]{2,1,0:T(8,128)S(1)} %bitcast.273), channel_id=1, source_target_pairs={{0,60},{4,0},{8,4},{12,8},{16,12},{20,16},{24,20},{28,24},{32,28},... | collective-permute-start | bytes 688136 | tf_op jit(solution)/shard_map/cond/branch_1_fun/ppermute | solution.py:27
  255.3 15.2 %all_to_all.107 = f32[4,112,128]{2,1,0:T(8,128)S(1)} all-to-all(f32[4,112,128]{2,1,0:T(8,128)S(1)} %maximum_add_fusion.3), channel_id=1, replica_groups={{0,16,32,48},{4,20,36,52},{8,24,40,56},{12,28,44,60},{1,17,33,49},{5,21..., dimensions={0} | all-to-all | bytes 458752 | tf_op jit(solution)/shard_map/cond/branch_1_fun/all_to_all | solution.py:18
  270.6 14.2 %all_to_all.108.own_ref = f32[16,112,128]{2,1,0:T(8,128)S(1)} all-to-all(f32[16,112,128]{2,1,0:T(8,128)S(1)} %broadcast_in_dim.118), channel_id=1, replica_groups={{0,1,2,3,128,129,130,131,256,257,258,259,384,385,386,387},{64,65,66,67,..., dimensions={0} | all-to-all | bytes 1835008 | tf_op jit(solution)/shard_map/cond/branch_1_fun/all_to_all | solution.py:18
  284.8 10.9 %collective-permute-start.15 = (f32[16,112,128]{2,1,0:T(8,128)S(1)}, f32[16,112,128]{2,1,0:T(8,128)S(1)}, u32[]{:S(2)}, u32[]{:S(2)}) collective-permute-start(f32[16,112,128]{2,1,0:T(8,128)S(1)} %all_to_all.108.own_ref), channel_id=1, source_target_pairs={{0,64},{64,0},{128,192},{192,128},{256,320},{320,256},{384,448},{4... | collective-permute-start | bytes 2752520 | tf_op jit(solution)/shard_map/cond/branch_1_fun/ppermute | solution.py:39
  297.8 7.3 %branch_1_fun.10 = f32[2304,128]{1,0:T(8,128)S(1)} custom-call(s32[320]{0:T(512)S(1)} %concatenate.44.info_ref, f32[16,112,128]{2,1,0:T(8,128)S(1)} %all_to_all.108.own_ref, f32[16,112,128]{2,1,0:T(8,128)S(1)} %collective-permute-done.15.other_ref), custom_call_target="tpu_custom_call" | custom-call | tf_op jit(solution)/shard_map/cond/branch_1_fun/pallas_call | solution.py:206
  326.5 22.7 %all_to_all.109 = f32[4,144,128]{2,1,0:T(8,128)S(1)} all-to-all(f32[4,144,128]{2,1,0:T(8,128)S(1)} %maximum_add_fusion), channel_id=1, replica_groups={{0,16,32,48},{4,20,36,52},{8,24,40,56},{12,28,44,60},{1,17,33,49},{5,21..., dimensions={0} | all-to-all | bytes 589824 | tf_op jit(solution)/shard_map/cond/branch_1_fun/all_to_all | solution.py:18
  355.7 13.6 %all_to_all.110 = f32[16,16,512]{2,1,0:T(8,128)S(1)} all-to-all(f32[16,16,512]{2,1,0:T(8,128)S(1)} %bitcast.245), channel_id=1, replica_groups={{0,1,2,3,128,129,130,131,256,257,258,259,384,385,386,387},{64,65,66,67,..., dimensions={0} | all-to-all | bytes 1048576 | tf_op jit(solution)/shard_map/cond/branch_1_fun/all_to_all | solution.py:18
  (160 shorter events, 103.1 us)
Async XLA Ops:
  2.8 18.3 %all-to-all-start.21 = ((f32[8,24,512]{2,1,0:T(8,128)}), f32[8,24,512]{2,1,0:T(8,128)S(1)}, u32[]{:S(2)}, u32[]{:S(2)}) async-start(f32[8,24,512]{2,1,0:T(8,128)} %bitcast.117), calls=%async_computation.21 | async-start | bytes 786432 | tf_op jit(solution)/shard_map/all_to_all | solution.py:18
  21.9 29.7 %copy-start.5 = (s32[4,2]{0,1:T(2,128)S(1)}, s32[4,2]{0,1:T(2,128)}, u32[]{:S(2)}) copy-start(s32[4,2]{0,1:T(2,128)} %param.10) | copy-start | bytes 100
  21.9 22.2 %all-to-all-start.22 = ((f32[16,8,128]{2,1,0:T(8,128)}), f32[16,8,128]{2,1,0:T(8,128)S(1)}, u32[]{:S(2)}, u32[]{:S(2)}) async-start(f32[16,8,128]{2,1,0:T(8,128)} %broadcast_in_dim.166), calls=%async_computation.22 | async-start | bytes 131072 | tf_op jit(solution)/shard_map/all_to_all | solution.py:18
  75.7 10.0 %collective-permute-start = (f32[16,144,128]{2,1,0:T(8,128)S(1)}, f32[16,144,128]{2,1,0:T(8,128)S(1)}, u32[]{:S(2)}, u32[]{:S(2)}) collective-permute-start(f32[16,144,128]{2,1,0:T(8,128)S(1)} %all_to_all.102.own_ref), channel_id=1, source_target_pairs={{0,64},{64,0},{128,192},{192,128},{256,320},{320,256},{384,448},{4... | collective-permute-start | bytes 3538952 | tf_op jit(solution)/shard_map/cond/branch_1_fun/ppermute | solution.py:39
  92.7 18.6 %collective-permute-start.1 = (f32[4,112,128]{2,1,0:T(8,128)S(1)}, f32[4,112,128]{2,1,0:T(8,128)S(1)}, u32[]{:S(2)}, u32[]{:S(2)}) collective-permute-start(f32[4,112,128]{2,1,0:T(8,128)S(1)} %bitcast.274), channel_id=1, source_target_pairs={{0,4},{4,8},{8,12},{12,16},{16,20},{20,24},{24,28},{28,32},{32,36}... | collective-permute-start | bytes 688136 | tf_op jit(solution)/shard_map/cond/branch_1_fun/ppermute | solution.py:27
  95.5 15.8 %collective-permute-start.2 = (f32[4,112,128]{2,1,0:T(8,128)S(1)}, f32[4,112,128]{2,1,0:T(8,128)S(1)}, u32[]{:S(2)}, u32[]{:S(2)}) collective-permute-start(f32[4,112,128]{2,1,0:T(8,128)S(1)} %bitcast.271), channel_id=1, source_target_pairs={{0,60},{4,0},{8,4},{12,8},{16,12},{20,16},{24,20},{28,24},{32,28},... | collective-permute-start | bytes 688136 | tf_op jit(solution)/shard_map/cond/branch_1_fun/ppermute | solution.py:27
  99.2 11.0 %collective-permute-start.3 = (f32[2,112,128]{2,1,0:T(8,128)S(1)}, f32[2,112,128]{2,1,0:T(8,128)S(1)}, u32[]{:S(2)}, u32[]{:S(2)}) collective-permute-start(f32[2,112,128]{2,1,0:T(8,128)S(1)} %bitcast.282), channel_id=1, source_target_pairs={{0,8},{4,12},{8,16},{12,20},{16,24},{20,28},{24,32},{28,36},{32,40... | collective-permute-start | bytes 344072 | tf_op jit(solution)/shard_map/cond/branch_1_fun/ppermute | solution.py:27
  101.2 10.1 %collective-permute-start.4 = (f32[2,112,128]{2,1,0:T(8,128)S(1)}, f32[2,112,128]{2,1,0:T(8,128)S(1)}, u32[]{:S(2)}, u32[]{:S(2)}) collective-permute-start(f32[2,112,128]{2,1,0:T(8,128)S(1)} %bitcast.279), channel_id=1, source_target_pairs={{0,56},{4,60},{8,0},{12,4},{16,8},{20,12},{24,16},{28,20},{32,24},... | collective-permute-start | bytes 344072 | tf_op jit(solution)/shard_map/cond/branch_1_fun/ppermute | solution.py:27
  144.9 9.6 %collective-permute-start.5 = (f32[16,112,128]{2,1,0:T(8,128)S(1)}, f32[16,112,128]{2,1,0:T(8,128)S(1)}, u32[]{:S(2)}, u32[]{:S(2)}) collective-permute-start(f32[16,112,128]{2,1,0:T(8,128)S(1)} %all_to_all.104.own_ref), channel_id=1, source_target_pairs={{0,64},{64,0},{128,192},{192,128},{256,320},{320,256},{384,448},{4... | collective-permute-start | bytes 2752520 | tf_op jit(solution)/shard_map/cond/branch_1_fun/ppermute | solution.py:39
  161.4 23.0 %collective-permute-start.6 = (f32[4,112,128]{2,1,0:T(8,128)S(1)}, f32[4,112,128]{2,1,0:T(8,128)S(1)}, u32[]{:S(2)}, u32[]{:S(2)}) collective-permute-start(f32[4,112,128]{2,1,0:T(8,128)S(1)} %bitcast.275), channel_id=1, source_target_pairs={{0,4},{4,8},{8,12},{12,16},{16,20},{20,24},{24,28},{28,32},{32,36}... | collective-permute-start | bytes 688136 | tf_op jit(solution)/shard_map/cond/branch_1_fun/ppermute | solution.py:27
  164.5 19.9 %collective-permute-start.7 = (f32[4,112,128]{2,1,0:T(8,128)S(1)}, f32[4,112,128]{2,1,0:T(8,128)S(1)}, u32[]{:S(2)}, u32[]{:S(2)}) collective-permute-start(f32[4,112,128]{2,1,0:T(8,128)S(1)} %bitcast.272), channel_id=1, source_target_pairs={{0,60},{4,0},{8,4},{12,8},{16,12},{20,16},{24,20},{28,24},{32,28},... | collective-permute-start | bytes 688136 | tf_op jit(solution)/shard_map/cond/branch_1_fun/ppermute | solution.py:27
  167.9 10.5 %collective-permute-start.8 = (f32[2,112,128]{2,1,0:T(8,128)S(1)}, f32[2,112,128]{2,1,0:T(8,128)S(1)}, u32[]{:S(2)}, u32[]{:S(2)}) collective-permute-start(f32[2,112,128]{2,1,0:T(8,128)S(1)} %bitcast.283), channel_id=1, source_target_pairs={{0,8},{4,12},{8,16},{12,20},{16,24},{20,28},{24,32},{28,36},{32,40... | collective-permute-start | bytes 344072 | tf_op jit(solution)/shard_map/cond/branch_1_fun/ppermute | solution.py:27
  174.5 9.9 %collective-permute-start.9 = (f32[2,112,128]{2,1,0:T(8,128)S(1)}, f32[2,112,128]{2,1,0:T(8,128)S(1)}, u32[]{:S(2)}, u32[]{:S(2)}) collective-permute-start(f32[2,112,128]{2,1,0:T(8,128)S(1)} %bitcast.280), channel_id=1, source_target_pairs={{0,56},{4,60},{8,0},{12,4},{16,8},{20,12},{24,16},{28,20},{32,24},... | collective-permute-start | bytes 344072 | tf_op jit(solution)/shard_map/cond/branch_1_fun/ppermute | solution.py:27
  214.5 11.8 %collective-permute-start.10 = (f32[16,112,128]{2,1,0:T(8,128)S(1)}, f32[16,112,128]{2,1,0:T(8,128)S(1)}, u32[]{:S(2)}, u32[]{:S(2)}) collective-permute-start(f32[16,112,128]{2,1,0:T(8,128)S(1)} %all_to_all.106.own_ref), channel_id=1, source_target_pairs={{0,64},{64,0},{128,192},{192,128},{256,320},{320,256},{384,448},{4... | collective-permute-start | bytes 2752520 | tf_op jit(solution)/shard_map/cond/branch_1_fun/ppermute | solution.py:39
  233.2 22.1 %collective-permute-start.11 = (f32[4,112,128]{2,1,0:T(8,128)S(1)}, f32[4,112,128]{2,1,0:T(8,128)S(1)}, u32[]{:S(2)}, u32[]{:S(2)}) collective-permute-start(f32[4,112,128]{2,1,0:T(8,128)S(1)} %bitcast.276), channel_id=1, source_target_pairs={{0,4},{4,8},{8,12},{12,16},{16,20},{20,24},{24,28},{28,32},{32,36}... | collective-permute-start | bytes 688136 | tf_op jit(solution)/shard_map/cond/branch_1_fun/ppermute | solution.py:27
  237.4 17.8 %collective-permute-start.12 = (f32[4,112,128]{2,1,0:T(8,128)S(1)}, f32[4,112,128]{2,1,0:T(8,128)S(1)}, u32[]{:S(2)}, u32[]{:S(2)}) collective-permute-start(f32[4,112,128]{2,1,0:T(8,128)S(1)} %bitcast.273), channel_id=1, source_target_pairs={{0,60},{4,0},{8,4},{12,8},{16,12},{20,16},{24,20},{28,24},{32,28},... | collective-permute-start | bytes 688136 | tf_op jit(solution)/shard_map/cond/branch_1_fun/ppermute | solution.py:27
  243.5 8.2 %collective-permute-start.13 = (f32[2,112,128]{2,1,0:T(8,128)S(1)}, f32[2,112,128]{2,1,0:T(8,128)S(1)}, u32[]{:S(2)}, u32[]{:S(2)}) collective-permute-start(f32[2,112,128]{2,1,0:T(8,128)S(1)} %bitcast.284), channel_id=1, source_target_pairs={{0,8},{4,12},{8,16},{12,20},{16,24},{20,28},{24,32},{28,36},{32,40... | collective-permute-start | bytes 344072 | tf_op jit(solution)/shard_map/cond/branch_1_fun/ppermute | solution.py:27
  245.4 9.8 %collective-permute-start.14 = (f32[2,112,128]{2,1,0:T(8,128)S(1)}, f32[2,112,128]{2,1,0:T(8,128)S(1)}, u32[]{:S(2)}, u32[]{:S(2)}) collective-permute-start(f32[2,112,128]{2,1,0:T(8,128)S(1)} %bitcast.281), channel_id=1, source_target_pairs={{0,56},{4,60},{8,0},{12,4},{16,8},{20,12},{24,16},{28,20},{32,24},... | collective-permute-start | bytes 344072 | tf_op jit(solution)/shard_map/cond/branch_1_fun/ppermute | solution.py:27
  284.8 13.0 %collective-permute-start.15 = (f32[16,112,128]{2,1,0:T(8,128)S(1)}, f32[16,112,128]{2,1,0:T(8,128)S(1)}, u32[]{:S(2)}, u32[]{:S(2)}) collective-permute-start(f32[16,112,128]{2,1,0:T(8,128)S(1)} %all_to_all.108.own_ref), channel_id=1, source_target_pairs={{0,64},{64,0},{128,192},{192,128},{256,320},{320,256},{384,448},{4... | collective-permute-start | bytes 2752520 | tf_op jit(solution)/shard_map/cond/branch_1_fun/ppermute | solution.py:39
  305.2 21.2 %collective-permute-start.16 = (f32[4,144,128]{2,1,0:T(8,128)S(1)}, f32[4,144,128]{2,1,0:T(8,128)S(1)}, u32[]{:S(2)}, u32[]{:S(2)}) collective-permute-start(f32[4,144,128]{2,1,0:T(8,128)S(1)} %bitcast.270), channel_id=1, source_target_pairs={{0,4},{4,8},{8,12},{12,16},{16,20},{20,24},{24,28},{28,32},{32,36}... | collective-permute-start | bytes 884744 | tf_op jit(solution)/shard_map/cond/branch_1_fun/ppermute | solution.py:27
  309.6 16.8 %collective-permute-start.17 = (f32[4,144,128]{2,1,0:T(8,128)S(1)}, f32[4,144,128]{2,1,0:T(8,128)S(1)}, u32[]{:S(2)}, u32[]{:S(2)}) collective-permute-start(f32[4,144,128]{2,1,0:T(8,128)S(1)} %bitcast.269), channel_id=1, source_target_pairs={{0,60},{4,0},{8,4},{12,8},{16,12},{20,16},{24,20},{28,24},{32,28},... | collective-permute-start | bytes 884744 | tf_op jit(solution)/shard_map/cond/branch_1_fun/ppermute | solution.py:27
  311.8 9.1 %collective-permute-start.18 = (f32[2,144,128]{2,1,0:T(8,128)S(1)}, f32[2,144,128]{2,1,0:T(8,128)S(1)}, u32[]{:S(2)}, u32[]{:S(2)}) collective-permute-start(f32[2,144,128]{2,1,0:T(8,128)S(1)} %bitcast.278), channel_id=1, source_target_pairs={{0,8},{4,12},{8,16},{12,20},{16,24},{20,28},{24,32},{28,36},{32,40... | collective-permute-start | bytes 442376 | tf_op jit(solution)/shard_map/cond/branch_1_fun/ppermute | solution.py:27
  315.2 11.2 %collective-permute-start.19 = (f32[2,144,128]{2,1,0:T(8,128)S(1)}, f32[2,144,128]{2,1,0:T(8,128)S(1)}, u32[]{:S(2)}, u32[]{:S(2)}) collective-permute-start(f32[2,144,128]{2,1,0:T(8,128)S(1)} %bitcast.277), channel_id=1, source_target_pairs={{0,56},{4,60},{8,0},{12,4},{16,8},{20,12},{24,16},{28,20},{32,24},... | collective-permute-start | bytes 442376 | tf_op jit(solution)/shard_map/cond/branch_1_fun/ppermute | solution.py:27
  349.2 5.0 %collective-permute-start.20 = (f32[144,128]{1,0:T(8,128)S(1)}, f32[144,128]{1,0:T(8,128)S(1)}, u32[]{:S(2)}, u32[]{:S(2)}) collective-permute-start(f32[144,128]{1,0:T(8,128)S(1)} %reduce_sum.135.own_ref), channel_id=1, source_target_pairs={{0,64},{64,0},{128,192},{192,128},{256,320},{320,256},{384,448},{4... | collective-permute-start | bytes 221192 | tf_op jit(solution)/shard_map/cond/branch_1_fun/ppermute | solution.py:39
  (5 other events, 114.3 us)
